TPU v7x, 32 devices: a whole 2x2x4 slice. The times are simulated.
32 devices in a mesh: groups: 2 (over x), blk: 16 (over z, y, core).
Axes of the slice: x: 2, y: 2, z: 4, core: 2. Of those that a mesh axis runs over, the one named last changes fastest.
Arguments:
- points: float32 [16384, 32], P(('groups', 'blk')), parts along dimension 0, may hold values from -6 to 6
- targets: float32 [16384, 16], P(('groups', 'blk')), parts along dimension 0, may hold values from -8 to 8
- noise_var: float32 [16384], P(('groups', 'blk')), parts along dimension 0, may hold values from 0.3 to 3
- inv_length: float32 [32], replicated, may hold values from 0.1 to 0.5
Outputs:
- solution: float32 [16384, 16], P(('groups', 'blk')), parts along dimension 0
- residual: float32 [16384, 16], P(('groups', 'blk')), parts along dimension 0
- direction: float32 [16384, 16], P(('groups', 'blk')), parts along dimension 0
There are 2 independent parts, one for each index of `groups`. A program takes and returns all parts, laid end to end along the dimension named above; an argument that names none is the same for every part. Nothing has to cross between parts.
All inputs are finite; a program needn't handle non-finite values.
Results may differ from a plain program's by a relative error of at most 0.0003.
Values sent between devices are 32-bit elements; how exact they have to be, the bound alone decides.
A program may use at most 64 MiB of HBM per device.

v0:
```python
import jax
import jax.numpy as jnp
from jax import lax
from jax.sharding import PartitionSpec as P


def shifted(value, axis, steps):
    count = lax.axis_size(axis)
    pairs = [(source, (source + steps) % count) for source in range(count)]
    return lax.ppermute(value, axis, pairs)


def product(left, right):
    return jnp.dot(left, right, precision=lax.Precision.HIGHEST, preferred_element_type=jnp.float32)


def kernel_tile(near, near_norms, far_points, far_norms):
    cross = lax.dot_general(
        near,
        far_points,
        (((1,), (1,)), ((), ())),
        precision=lax.Precision.HIGHEST,
        preferred_element_type=jnp.float32,
    )
    return jnp.exp(-0.5 * (near_norms[:, None] + far_norms[None, :] - 2.0 * cross))


def body(points, targets, noise_var, inv_length):
    cycle_size = lax.axis_size("blk")
    scaled = points * inv_length[None, :]
    sqnorm = jnp.sum(scaled * scaled, axis=1)

    def column_norms(residual):
        return lax.psum(jnp.sum(residual * residual, axis=0), "blk")

    residual = targets
    direction = targets
    norm_now = column_norms(residual)
    accumulated = product(kernel_tile(scaled, sqnorm, scaled, sqnorm), direction)

    def visit_block(step_index, state_tuple):
        accumulated, far_points, far_norms, incoming = state_tuple
        far_points, far_norms, incoming = shifted((far_points, far_norms, incoming), "blk", 1)
        tile_values = kernel_tile(scaled, sqnorm, far_points, far_norms)
        return (accumulated + product(tile_values, incoming), far_points, far_norms, incoming)

    accumulated = lax.fori_loop(
        1, cycle_size, visit_block, (accumulated, scaled, sqnorm, direction)
    )[0]
    image = accumulated + noise_var[:, None] * direction
    curvature = lax.psum(jnp.sum(direction * image, axis=0), "blk")
    step_size = norm_now / curvature
    solution = step_size[None, :] * direction
    residual = residual - step_size[None, :] * image
    norm_next = column_norms(residual)
    direction = residual + (norm_next / norm_now)[None, :] * direction
    return (solution, residual, direction)


def solution(mesh):
    placed = (P(("groups", "blk"), None), P(("groups", "blk"), None), P(("groups", "blk")), P())
    return jax.shard_map(
        body,
        mesh=mesh,
        in_specs=placed,
        out_specs=(
            P(("groups", "blk"), None),
            P(("groups", "blk"), None),
            P(("groups", "blk"), None),
        ),
        check_vma=False,
    )
```

profile of v0, /device:TPU:0, one launch (start us, length us, event | category | flops | bytes accessed | tf_op | source)
XLA Modules:
  0.0 234.0 jit_solution(14439315354553758097)
XLA Ops:
  1.8 1.1 fusion.10
  2.9 1.0 fusion.11
  4.7 168.6 %while.16 = (s32[]{:T(128)}, f32[512,16]{0,1:T(8,128)S(1)}, f32[512,32]{1,0:T(8,128)S(1)}, f32[512]{0:T(512)S(1)}, f32[512,16]{0,1:T(8,128)S(1)}, /*index=5*/f32[512]{0:T(512)S(1)}, f32[512,32]{1,0:T(8,128)S(1)}, s32[]{:T(128)}) while((s32[]{:T(128)}, f32[512,16]{0,1:T(8,128)S(1)}, f32[512,32]{1,0:T(8,128)S(1)}, f32[512]{0:T(512)S(1)}, ...), condition=%wide.region_4.0_spmd, body=%wide.region_3.0_spmd.sunk | while | flops 152051712 | bytes 2932941 | solution.py:47
  5.2 2.6 %collective-permute-start = (f32[512,16]{0,1:T(8,128)S(1)}, f32[512,16]{0,1:T(8,128)S(1)}, u32[]{:S(2)}, u32[]{:S(2)}) collective-permute-start(f32[512,16]{0,1:T(8,128)S(1)} %get-tuple-element.119), channel_id=1, source_target_pairs={{0,1},{1,2},{2,3},{3,4},{4,5},{5,6},{6,7},{7,8},{8,9},{9,10},{10,1... | collective-permute-start | bytes 98312 | tf_op jit(solution)/shard_map/while/body/eval_jaxpr/ppermute | solution.py:10
  7.9 6.8 %collective-permute-done.2 = f32[512]{0:T(512)S(1)} collective-permute-done((f32[512]{0:T(512)S(1)}, f32[512]{0:T(512)S(1)}, u32[]{:S(2)}, u32[]{:S(2)}) %collective-permute-start.2) | collective-permute-done | bytes 2080 | tf_op jit(solution)/shard_map/while/body/eval_jaxpr/ppermute | solution.py:10
  14.7 1.0 convolution_multiply_fusion.3
  15.7 1.2 convolution_add_fusion.2
  17.1 8.7 %collective-permute-done.2 = f32[512]{0:T(512)S(1)} collective-permute-done((f32[512]{0:T(512)S(1)}, f32[512]{0:T(512)S(1)}, u32[]{:S(2)}, u32[]{:S(2)}) %collective-permute-start.2) | collective-permute-done | bytes 2080 | tf_op jit(solution)/shard_map/while/body/eval_jaxpr/ppermute | solution.py:10
  25.8 1.0 convolution_multiply_fusion.3
  26.8 1.2 convolution_add_fusion.2
  28.2 8.7 %collective-permute-done.2 = f32[512]{0:T(512)S(1)} collective-permute-done((f32[512]{0:T(512)S(1)}, f32[512]{0:T(512)S(1)}, u32[]{:S(2)}, u32[]{:S(2)}) %collective-permute-start.2) | collective-permute-done | bytes 2080 | tf_op jit(solution)/shard_map/while/body/eval_jaxpr/ppermute | solution.py:10
  38.0 1.2 convolution_add_fusion.2
  39.4 8.7 %collective-permute-done.2 = f32[512]{0:T(512)S(1)} collective-permute-done((f32[512]{0:T(512)S(1)}, f32[512]{0:T(512)S(1)}, u32[]{:S(2)}, u32[]{:S(2)}) %collective-permute-start.2) | collective-permute-done | bytes 2080 | tf_op jit(solution)/shard_map/while/body/eval_jaxpr/ppermute | solution.py:10
  49.2 1.2 convolution_add_fusion.2
  50.6 8.7 %collective-permute-done.2 = f32[512]{0:T(512)S(1)} collective-permute-done((f32[512]{0:T(512)S(1)}, f32[512]{0:T(512)S(1)}, u32[]{:S(2)}, u32[]{:S(2)}) %collective-permute-start.2) | collective-permute-done | bytes 2080 | tf_op jit(solution)/shard_map/while/body/eval_jaxpr/ppermute | solution.py:10
  59.3 1.0 convolution_multiply_fusion.3
  60.3 1.2 convolution_add_fusion.2
  61.7 8.7 %collective-permute-done.2 = f32[512]{0:T(512)S(1)} collective-permute-done((f32[512]{0:T(512)S(1)}, f32[512]{0:T(512)S(1)}, u32[]{:S(2)}, u32[]{:S(2)}) %collective-permute-start.2) | collective-permute-done | bytes 2080 | tf_op jit(solution)/shard_map/while/body/eval_jaxpr/ppermute | solution.py:10
  70.5 1.0 convolution_multiply_fusion.3
  71.5 1.2 convolution_add_fusion.2
  72.9 8.7 %collective-permute-done.2 = f32[512]{0:T(512)S(1)} collective-permute-done((f32[512]{0:T(512)S(1)}, f32[512]{0:T(512)S(1)}, u32[]{:S(2)}, u32[]{:S(2)}) %collective-permute-start.2) | collective-permute-done | bytes 2080 | tf_op jit(solution)/shard_map/while/body/eval_jaxpr/ppermute | solution.py:10
  81.7 1.0 convolution_multiply_fusion.3
  82.7 1.2 convolution_add_fusion.2
  84.1 8.7 %collective-permute-done.2 = f32[512]{0:T(512)S(1)} collective-permute-done((f32[512]{0:T(512)S(1)}, f32[512]{0:T(512)S(1)}, u32[]{:S(2)}, u32[]{:S(2)}) %collective-permute-start.2) | collective-permute-done | bytes 2080 | tf_op jit(solution)/shard_map/while/body/eval_jaxpr/ppermute | solution.py:10
  92.9 1.0 convolution_multiply_fusion.3
  93.9 1.2 convolution_add_fusion.2
  95.3 8.7 %collective-permute-done.2 = f32[512]{0:T(512)S(1)} collective-permute-done((f32[512]{0:T(512)S(1)}, f32[512]{0:T(512)S(1)}, u32[]{:S(2)}, u32[]{:S(2)}) %collective-permute-start.2) | collective-permute-done | bytes 2080 | tf_op jit(solution)/shard_map/while/body/eval_jaxpr/ppermute | solution.py:10
  104.0 1.0 convolution_multiply_fusion.3
  105.0 1.2 convolution_add_fusion.2
  106.4 8.7 %collective-permute-done.2 = f32[512]{0:T(512)S(1)} collective-permute-done((f32[512]{0:T(512)S(1)}, f32[512]{0:T(512)S(1)}, u32[]{:S(2)}, u32[]{:S(2)}) %collective-permute-start.2) | collective-permute-done | bytes 2080 | tf_op jit(solution)/shard_map/while/body/eval_jaxpr/ppermute | solution.py:10
  115.2 1.0 convolution_multiply_fusion.3
  116.2 1.2 convolution_add_fusion.2
  117.6 8.7 %collective-permute-done.2 = f32[512]{0:T(512)S(1)} collective-permute-done((f32[512]{0:T(512)S(1)}, f32[512]{0:T(512)S(1)}, u32[]{:S(2)}, u32[]{:S(2)}) %collective-permute-start.2) | collective-permute-done | bytes 2080 | tf_op jit(solution)/shard_map/while/body/eval_jaxpr/ppermute | solution.py:10
  126.4 1.0 convolution_multiply_fusion.3
  127.4 1.2 convolution_add_fusion.2
  128.8 8.7 %collective-permute-done.2 = f32[512]{0:T(512)S(1)} collective-permute-done((f32[512]{0:T(512)S(1)}, f32[512]{0:T(512)S(1)}, u32[]{:S(2)}, u32[]{:S(2)}) %collective-permute-start.2) | collective-permute-done | bytes 2080 | tf_op jit(solution)/shard_map/while/body/eval_jaxpr/ppermute | solution.py:10
  137.6 1.0 convolution_multiply_fusion.3
  138.6 1.2 convolution_add_fusion.2
  140.0 8.7 %collective-permute-done.2 = f32[512]{0:T(512)S(1)} collective-permute-done((f32[512]{0:T(512)S(1)}, f32[512]{0:T(512)S(1)}, u32[]{:S(2)}, u32[]{:S(2)}) %collective-permute-start.2) | collective-permute-done | bytes 2080 | tf_op jit(solution)/shard_map/while/body/eval_jaxpr/ppermute | solution.py:10
  148.7 1.0 convolution_multiply_fusion.3
  149.7 1.2 convolution_add_fusion.2
  151.1 8.7 %collective-permute-done.2 = f32[512]{0:T(512)S(1)} collective-permute-done((f32[512]{0:T(512)S(1)}, f32[512]{0:T(512)S(1)}, u32[]{:S(2)}, u32[]{:S(2)}) %collective-permute-start.2) | collective-permute-done | bytes 2080 | tf_op jit(solution)/shard_map/while/body/eval_jaxpr/ppermute | solution.py:10
  159.9 1.0 convolution_multiply_fusion.3
  160.9 1.2 convolution_add_fusion.2
  162.3 8.8 %collective-permute-done.2 = f32[512]{0:T(512)S(1)} collective-permute-done((f32[512]{0:T(512)S(1)}, f32[512]{0:T(512)S(1)}, u32[]{:S(2)}, u32[]{:S(2)}) %collective-permute-start.2) | collective-permute-done | bytes 2080 | tf_op jit(solution)/shard_map/while/body/eval_jaxpr/ppermute | solution.py:10
  172.1 1.2 convolution_add_fusion.2
  173.5 29.5 %all-reduce = (f32[16]{0:T(128)S(1)}, f32[16]{0:T(128)S(1)}) all-reduce(f32[16]{0:T(128)S(1)} %get-tuple-element.42, f32[16]{0:T(128)S(1)} %get-tuple-element.41), channel_id=1, replica_groups=mesh['groups'=2,'blk'=16] {'blk'}, use_global_device_ids=true, to_apply=%region_1.0 | all-reduce | flops 32 | bytes 256 | tf_op jit(solution)/shard_map/psum | solution.py:34
  203.8 29.5 %psum.23 = f32[16]{0:T(128)S(1)} all-reduce(f32[16]{0:T(128)S(1)} %get-tuple-element.59), channel_id=1, replica_groups=mesh['groups'=2,'blk'=16] {'blk'}, use_global_device_ids=true, to_apply=%region_8.0 | all-reduce | flops 16 | bytes 128 | tf_op jit(solution)/shard_map/psum | solution.py:34
  (141 shorter events, 9.7 us)
Async XLA Ops:
  1.8 1.2 copy-start
  4.7 168.6 %copy-start.3 = (f32[512]{0:T(512)S(1)}, f32[512]{0:T(512)}, u32[]{:S(2)}) copy-start(f32[512]{0:T(512)} %param.8) | copy-start | bytes 6148
  4.7 9.9 %collective-permute-start.1 = (f32[512,32]{1,0:T(8,128)S(1)}, f32[512,32]{1,0:T(8,128)S(1)}, u32[]{:S(2)}, u32[]{:S(2)}) collective-permute-start(f32[512,32]{1,0:T(8,128)S(1)} %get-tuple-element.117), channel_id=1, source_target_pairs={{0,1},{1,2},{2,3},{3,4},{4,5},{5,6},{6,7},{7,8},{8,9},{9,10},{10,1... | collective-permute-start | bytes 196616 | tf_op jit(solution)/shard_map/while/body/eval_jaxpr/ppermute | solution.py:10
  5.2 9.4 %collective-permute-start = (f32[512,16]{0,1:T(8,128)S(1)}, f32[512,16]{0,1:T(8,128)S(1)}, u32[]{:S(2)}, u32[]{:S(2)}) collective-permute-start(f32[512,16]{0,1:T(8,128)S(1)} %get-tuple-element.119), channel_id=1, source_target_pairs={{0,1},{1,2},{2,3},{3,4},{4,5},{5,6},{6,7},{7,8},{8,9},{9,10},{10,1... | collective-permute-start | bytes 98312 | tf_op jit(solution)/shard_map/while/body/eval_jaxpr/ppermute | solution.py:10
  7.8 6.8 %collective-permute-start.2 = (f32[512]{0:T(512)S(1)}, f32[512]{0:T(512)S(1)}, u32[]{:S(2)}, u32[]{:S(2)}) collective-permute-start(f32[512]{0:T(512)S(1)} %get-tuple-element.118), channel_id=1, source_target_pairs={{0,1},{1,2},{2,3},{3,4},{4,5},{5,6},{6,7},{7,8},{8,9},{9,10},{10,1... | collective-permute-start | bytes 6152 | tf_op jit(solution)/shard_map/while/body/eval_jaxpr/ppermute | solution.py:10
  16.9 8.9 %collective-permute-start.1 = (f32[512,32]{1,0:T(8,128)S(1)}, f32[512,32]{1,0:T(8,128)S(1)}, u32[]{:S(2)}, u32[]{:S(2)}) collective-permute-start(f32[512,32]{1,0:T(8,128)S(1)} %get-tuple-element.117), channel_id=1, source_target_pairs={{0,1},{1,2},{2,3},{3,4},{4,5},{5,6},{6,7},{7,8},{8,9},{9,10},{10,1... | collective-permute-start | bytes 196616 | tf_op jit(solution)/shard_map/while/body/eval_jaxpr/ppermute | solution.py:10
  16.9 8.9 %collective-permute-start = (f32[512,16]{0,1:T(8,128)S(1)}, f32[512,16]{0,1:T(8,128)S(1)}, u32[]{:S(2)}, u32[]{:S(2)}) collective-permute-start(f32[512,16]{0,1:T(8,128)S(1)} %get-tuple-element.119), channel_id=1, source_target_pairs={{0,1},{1,2},{2,3},{3,4},{4,5},{5,6},{6,7},{7,8},{8,9},{9,10},{10,1... | collective-permute-start | bytes 98312 | tf_op jit(solution)/shard_map/while/body/eval_jaxpr/ppermute | solution.py:10
  17.0 8.8 %collective-permute-start.2 = (f32[512]{0:T(512)S(1)}, f32[512]{0:T(512)S(1)}, u32[]{:S(2)}, u32[]{:S(2)}) collective-permute-start(f32[512]{0:T(512)S(1)} %get-tuple-element.118), channel_id=1, source_target_pairs={{0,1},{1,2},{2,3},{3,4},{4,5},{5,6},{6,7},{7,8},{8,9},{9,10},{10,1... | collective-permute-start | bytes 6152 | tf_op jit(solution)/shard_map/while/body/eval_jaxpr/ppermute | solution.py:10
  28.0 8.9 %collective-permute-start.1 = (f32[512,32]{1,0:T(8,128)S(1)}, f32[512,32]{1,0:T(8,128)S(1)}, u32[]{:S(2)}, u32[]{:S(2)}) collective-permute-start(f32[512,32]{1,0:T(8,128)S(1)} %get-tuple-element.117), channel_id=1, source_target_pairs={{0,1},{1,2},{2,3},{3,4},{4,5},{5,6},{6,7},{7,8},{8,9},{9,10},{10,1... | collective-permute-start | bytes 196616 | tf_op jit(solution)/shard_map/while/body/eval_jaxpr/ppermute | solution.py:10
  28.1 8.9 %collective-permute-start = (f32[512,16]{0,1:T(8,128)S(1)}, f32[512,16]{0,1:T(8,128)S(1)}, u32[]{:S(2)}, u32[]{:S(2)}) collective-permute-start(f32[512,16]{0,1:T(8,128)S(1)} %get-tuple-element.119), channel_id=1, source_target_pairs={{0,1},{1,2},{2,3},{3,4},{4,5},{5,6},{6,7},{7,8},{8,9},{9,10},{10,1... | collective-permute-start | bytes 98312 | tf_op jit(solution)/shard_map/while/body/eval_jaxpr/ppermute | solution.py:10
  28.2 8.8 %collective-permute-start.2 = (f32[512]{0:T(512)S(1)}, f32[512]{0:T(512)S(1)}, u32[]{:S(2)}, u32[]{:S(2)}) collective-permute-start(f32[512]{0:T(512)S(1)} %get-tuple-element.118), channel_id=1, source_target_pairs={{0,1},{1,2},{2,3},{3,4},{4,5},{5,6},{6,7},{7,8},{8,9},{9,10},{10,1... | collective-permute-start | bytes 6152 | tf_op jit(solution)/shard_map/while/body/eval_jaxpr/ppermute | solution.py:10
  39.2 8.9 %collective-permute-start.1 = (f32[512,32]{1,0:T(8,128)S(1)}, f32[512,32]{1,0:T(8,128)S(1)}, u32[]{:S(2)}, u32[]{:S(2)}) collective-permute-start(f32[512,32]{1,0:T(8,128)S(1)} %get-tuple-element.117), channel_id=1, source_target_pairs={{0,1},{1,2},{2,3},{3,4},{4,5},{5,6},{6,7},{7,8},{8,9},{9,10},{10,1... | collective-permute-start | bytes 196616 | tf_op jit(solution)/shard_map/while/body/eval_jaxpr/ppermute | solution.py:10
  39.3 8.9 %collective-permute-start = (f32[512,16]{0,1:T(8,128)S(1)}, f32[512,16]{0,1:T(8,128)S(1)}, u32[]{:S(2)}, u32[]{:S(2)}) collective-permute-start(f32[512,16]{0,1:T(8,128)S(1)} %get-tuple-element.119), channel_id=1, source_target_pairs={{0,1},{1,2},{2,3},{3,4},{4,5},{5,6},{6,7},{7,8},{8,9},{9,10},{10,1... | collective-permute-start | bytes 98312 | tf_op jit(solution)/shard_map/while/body/eval_jaxpr/ppermute | solution.py:10
  39.3 8.8 %collective-permute-start.2 = (f32[512]{0:T(512)S(1)}, f32[512]{0:T(512)S(1)}, u32[]{:S(2)}, u32[]{:S(2)}) collective-permute-start(f32[512]{0:T(512)S(1)} %get-tuple-element.118), channel_id=1, source_target_pairs={{0,1},{1,2},{2,3},{3,4},{4,5},{5,6},{6,7},{7,8},{8,9},{9,10},{10,1... | collective-permute-start | bytes 6152 | tf_op jit(solution)/shard_map/while/body/eval_jaxpr/ppermute | solution.py:10
  50.4 8.9 %collective-permute-start.1 = (f32[512,32]{1,0:T(8,128)S(1)}, f32[512,32]{1,0:T(8,128)S(1)}, u32[]{:S(2)}, u32[]{:S(2)}) collective-permute-start(f32[512,32]{1,0:T(8,128)S(1)} %get-tuple-element.117), channel_id=1, source_target_pairs={{0,1},{1,2},{2,3},{3,4},{4,5},{5,6},{6,7},{7,8},{8,9},{9,10},{10,1... | collective-permute-start | bytes 196616 | tf_op jit(solution)/shard_map/while/body/eval_jaxpr/ppermute | solution.py:10
  50.4 8.9 %collective-permute-start = (f32[512,16]{0,1:T(8,128)S(1)}, f32[512,16]{0,1:T(8,128)S(1)}, u32[]{:S(2)}, u32[]{:S(2)}) collective-permute-start(f32[512,16]{0,1:T(8,128)S(1)} %get-tuple-element.119), channel_id=1, source_target_pairs={{0,1},{1,2},{2,3},{3,4},{4,5},{5,6},{6,7},{7,8},{8,9},{9,10},{10,1... | collective-permute-start | bytes 98312 | tf_op jit(solution)/shard_map/while/body/eval_jaxpr/ppermute | solution.py:10
  50.5 8.8 %collective-permute-start.2 = (f32[512]{0:T(512)S(1)}, f32[512]{0:T(512)S(1)}, u32[]{:S(2)}, u32[]{:S(2)}) collective-permute-start(f32[512]{0:T(512)S(1)} %get-tuple-element.118), channel_id=1, source_target_pairs={{0,1},{1,2},{2,3},{3,4},{4,5},{5,6},{6,7},{7,8},{8,9},{9,10},{10,1... | collective-permute-start | bytes 6152 | tf_op jit(solution)/shard_map/while/body/eval_jaxpr/ppermute | solution.py:10
  61.6 8.9 %collective-permute-start.1 = (f32[512,32]{1,0:T(8,128)S(1)}, f32[512,32]{1,0:T(8,128)S(1)}, u32[]{:S(2)}, u32[]{:S(2)}) collective-permute-start(f32[512,32]{1,0:T(8,128)S(1)} %get-tuple-element.117), channel_id=1, source_target_pairs={{0,1},{1,2},{2,3},{3,4},{4,5},{5,6},{6,7},{7,8},{8,9},{9,10},{10,1... | collective-permute-start | bytes 196616 | tf_op jit(solution)/shard_map/while/body/eval_jaxpr/ppermute | solution.py:10
  61.6 8.9 %collective-permute-start = (f32[512,16]{0,1:T(8,128)S(1)}, f32[512,16]{0,1:T(8,128)S(1)}, u32[]{:S(2)}, u32[]{:S(2)}) collective-permute-start(f32[512,16]{0,1:T(8,128)S(1)} %get-tuple-element.119), channel_id=1, source_target_pairs={{0,1},{1,2},{2,3},{3,4},{4,5},{5,6},{6,7},{7,8},{8,9},{9,10},{10,1... | collective-permute-start | bytes 98312 | tf_op jit(solution)/shard_map/while/body/eval_jaxpr/ppermute | solution.py:10
  61.7 8.8 %collective-permute-start.2 = (f32[512]{0:T(512)S(1)}, f32[512]{0:T(512)S(1)}, u32[]{:S(2)}, u32[]{:S(2)}) collective-permute-start(f32[512]{0:T(512)S(1)} %get-tuple-element.118), channel_id=1, source_target_pairs={{0,1},{1,2},{2,3},{3,4},{4,5},{5,6},{6,7},{7,8},{8,9},{9,10},{10,1... | collective-permute-start | bytes 6152 | tf_op jit(solution)/shard_map/while/body/eval_jaxpr/ppermute | solution.py:10
  72.7 8.9 %collective-permute-start.1 = (f32[512,32]{1,0:T(8,128)S(1)}, f32[512,32]{1,0:T(8,128)S(1)}, u32[]{:S(2)}, u32[]{:S(2)}) collective-permute-start(f32[512,32]{1,0:T(8,128)S(1)} %get-tuple-element.117), channel_id=1, source_target_pairs={{0,1},{1,2},{2,3},{3,4},{4,5},{5,6},{6,7},{7,8},{8,9},{9,10},{10,1... | collective-permute-start | bytes 196616 | tf_op jit(solution)/shard_map/while/body/eval_jaxpr/ppermute | solution.py:10
  72.8 8.9 %collective-permute-start = (f32[512,16]{0,1:T(8,128)S(1)}, f32[512,16]{0,1:T(8,128)S(1)}, u32[]{:S(2)}, u32[]{:S(2)}) collective-permute-start(f32[512,16]{0,1:T(8,128)S(1)} %get-tuple-element.119), channel_id=1, source_target_pairs={{0,1},{1,2},{2,3},{3,4},{4,5},{5,6},{6,7},{7,8},{8,9},{9,10},{10,1... | collective-permute-start | bytes 98312 | tf_op jit(solution)/shard_map/while/body/eval_jaxpr/ppermute | solution.py:10
  72.8 8.8 %collective-permute-start.2 = (f32[512]{0:T(512)S(1)}, f32[512]{0:T(512)S(1)}, u32[]{:S(2)}, u32[]{:S(2)}) collective-permute-start(f32[512]{0:T(512)S(1)} %get-tuple-element.118), channel_id=1, source_target_pairs={{0,1},{1,2},{2,3},{3,4},{4,5},{5,6},{6,7},{7,8},{8,9},{9,10},{10,1... | collective-permute-start | bytes 6152 | tf_op jit(solution)/shard_map/while/body/eval_jaxpr/ppermute | solution.py:10
  83.9 8.9 %collective-permute-start.1 = (f32[512,32]{1,0:T(8,128)S(1)}, f32[512,32]{1,0:T(8,128)S(1)}, u32[]{:S(2)}, u32[]{:S(2)}) collective-permute-start(f32[512,32]{1,0:T(8,128)S(1)} %get-tuple-element.117), channel_id=1, source_target_pairs={{0,1},{1,2},{2,3},{3,4},{4,5},{5,6},{6,7},{7,8},{8,9},{9,10},{10,1... | collective-permute-start | bytes 196616 | tf_op jit(solution)/shard_map/while/body/eval_jaxpr/ppermute | solution.py:10
  84.0 8.9 %collective-permute-start = (f32[512,16]{0,1:T(8,128)S(1)}, f32[512,16]{0,1:T(8,128)S(1)}, u32[]{:S(2)}, u32[]{:S(2)}) collective-permute-start(f32[512,16]{0,1:T(8,128)S(1)} %get-tuple-element.119), channel_id=1, source_target_pairs={{0,1},{1,2},{2,3},{3,4},{4,5},{5,6},{6,7},{7,8},{8,9},{9,10},{10,1... | collective-permute-start | bytes 98312 | tf_op jit(solution)/shard_map/while/body/eval_jaxpr/ppermute | solution.py:10
  84.0 8.8 %collective-permute-start.2 = (f32[512]{0:T(512)S(1)}, f32[512]{0:T(512)S(1)}, u32[]{:S(2)}, u32[]{:S(2)}) collective-permute-start(f32[512]{0:T(512)S(1)} %get-tuple-element.118), channel_id=1, source_target_pairs={{0,1},{1,2},{2,3},{3,4},{4,5},{5,6},{6,7},{7,8},{8,9},{9,10},{10,1... | collective-permute-start | bytes 6152 | tf_op jit(solution)/shard_map/while/body/eval_jaxpr/ppermute | solution.py:10
  95.1 8.9 %collective-permute-start.1 = (f32[512,32]{1,0:T(8,128)S(1)}, f32[512,32]{1,0:T(8,128)S(1)}, u32[]{:S(2)}, u32[]{:S(2)}) collective-permute-start(f32[512,32]{1,0:T(8,128)S(1)} %get-tuple-element.117), channel_id=1, source_target_pairs={{0,1},{1,2},{2,3},{3,4},{4,5},{5,6},{6,7},{7,8},{8,9},{9,10},{10,1... | collective-permute-start | bytes 196616 | tf_op jit(solution)/shard_map/while/body/eval_jaxpr/ppermute | solution.py:10
  95.1 8.9 %collective-permute-start = (f32[512,16]{0,1:T(8,128)S(1)}, f32[512,16]{0,1:T(8,128)S(1)}, u32[]{:S(2)}, u32[]{:S(2)}) collective-permute-start(f32[512,16]{0,1:T(8,128)S(1)} %get-tuple-element.119), channel_id=1, source_target_pairs={{0,1},{1,2},{2,3},{3,4},{4,5},{5,6},{6,7},{7,8},{8,9},{9,10},{10,1... | collective-permute-start | bytes 98312 | tf_op jit(solution)/shard_map/while/body/eval_jaxpr/ppermute | solution.py:10
  95.2 8.8 %collective-permute-start.2 = (f32[512]{0:T(512)S(1)}, f32[512]{0:T(512)S(1)}, u32[]{:S(2)}, u32[]{:S(2)}) collective-permute-start(f32[512]{0:T(512)S(1)} %get-tuple-element.118), channel_id=1, source_target_pairs={{0,1},{1,2},{2,3},{3,4},{4,5},{5,6},{6,7},{7,8},{8,9},{9,10},{10,1... | collective-permute-start | bytes 6152 | tf_op jit(solution)/shard_map/while/body/eval_jaxpr/ppermute | solution.py:10
  106.2 8.9 %collective-permute-start.1 = (f32[512,32]{1,0:T(8,128)S(1)}, f32[512,32]{1,0:T(8,128)S(1)}, u32[]{:S(2)}, u32[]{:S(2)}) collective-permute-start(f32[512,32]{1,0:T(8,128)S(1)} %get-tuple-element.117), channel_id=1, source_target_pairs={{0,1},{1,2},{2,3},{3,4},{4,5},{5,6},{6,7},{7,8},{8,9},{9,10},{10,1... | collective-permute-start | bytes 196616 | tf_op jit(solution)/shard_map/while/body/eval_jaxpr/ppermute | solution.py:10
  106.3 8.9 %collective-permute-start = (f32[512,16]{0,1:T(8,128)S(1)}, f32[512,16]{0,1:T(8,128)S(1)}, u32[]{:S(2)}, u32[]{:S(2)}) collective-permute-start(f32[512,16]{0,1:T(8,128)S(1)} %get-tuple-element.119), channel_id=1, source_target_pairs={{0,1},{1,2},{2,3},{3,4},{4,5},{5,6},{6,7},{7,8},{8,9},{9,10},{10,1... | collective-permute-start | bytes 98312 | tf_op jit(solution)/shard_map/while/body/eval_jaxpr/ppermute | solution.py:10
  106.4 8.8 %collective-permute-start.2 = (f32[512]{0:T(512)S(1)}, f32[512]{0:T(512)S(1)}, u32[]{:S(2)}, u32[]{:S(2)}) collective-permute-start(f32[512]{0:T(512)S(1)} %get-tuple-element.118), channel_id=1, source_target_pairs={{0,1},{1,2},{2,3},{3,4},{4,5},{5,6},{6,7},{7,8},{8,9},{9,10},{10,1... | collective-permute-start | bytes 6152 | tf_op jit(solution)/shard_map/while/body/eval_jaxpr/ppermute | solution.py:10
  117.4 8.9 %collective-permute-start.1 = (f32[512,32]{1,0:T(8,128)S(1)}, f32[512,32]{1,0:T(8,128)S(1)}, u32[]{:S(2)}, u32[]{:S(2)}) collective-permute-start(f32[512,32]{1,0:T(8,128)S(1)} %get-tuple-element.117), channel_id=1, source_target_pairs={{0,1},{1,2},{2,3},{3,4},{4,5},{5,6},{6,7},{7,8},{8,9},{9,10},{10,1... | collective-permute-start | bytes 196616 | tf_op jit(solution)/shard_map/while/body/eval_jaxpr/ppermute | solution.py:10
  117.5 8.9 %collective-permute-start = (f32[512,16]{0,1:T(8,128)S(1)}, f32[512,16]{0,1:T(8,128)S(1)}, u32[]{:S(2)}, u32[]{:S(2)}) collective-permute-start(f32[512,16]{0,1:T(8,128)S(1)} %get-tuple-element.119), channel_id=1, source_target_pairs={{0,1},{1,2},{2,3},{3,4},{4,5},{5,6},{6,7},{7,8},{8,9},{9,10},{10,1... | collective-permute-start | bytes 98312 | tf_op jit(solution)/shard_map/while/body/eval_jaxpr/ppermute | solution.py:10
  117.5 8.8 %collective-permute-start.2 = (f32[512]{0:T(512)S(1)}, f32[512]{0:T(512)S(1)}, u32[]{:S(2)}, u32[]{:S(2)}) collective-permute-start(f32[512]{0:T(512)S(1)} %get-tuple-element.118), channel_id=1, source_target_pairs={{0,1},{1,2},{2,3},{3,4},{4,5},{5,6},{6,7},{7,8},{8,9},{9,10},{10,1... | collective-permute-start | bytes 6152 | tf_op jit(solution)/shard_map/while/body/eval_jaxpr/ppermute | solution.py:10
  128.6 8.9 %collective-permute-start.1 = (f32[512,32]{1,0:T(8,128)S(1)}, f32[512,32]{1,0:T(8,128)S(1)}, u32[]{:S(2)}, u32[]{:S(2)}) collective-permute-start(f32[512,32]{1,0:T(8,128)S(1)} %get-tuple-element.117), channel_id=1, source_target_pairs={{0,1},{1,2},{2,3},{3,4},{4,5},{5,6},{6,7},{7,8},{8,9},{9,10},{10,1... | collective-permute-start | bytes 196616 | tf_op jit(solution)/shard_map/while/body/eval_jaxpr/ppermute | solution.py:10
  128.7 8.9 %collective-permute-start = (f32[512,16]{0,1:T(8,128)S(1)}, f32[512,16]{0,1:T(8,128)S(1)}, u32[]{:S(2)}, u32[]{:S(2)}) collective-permute-start(f32[512,16]{0,1:T(8,128)S(1)} %get-tuple-element.119), channel_id=1, source_target_pairs={{0,1},{1,2},{2,3},{3,4},{4,5},{5,6},{6,7},{7,8},{8,9},{9,10},{10,1... | collective-permute-start | bytes 98312 | tf_op jit(solution)/shard_map/while/body/eval_jaxpr/ppermute | solution.py:10
  128.7 8.8 %collective-permute-start.2 = (f32[512]{0:T(512)S(1)}, f32[512]{0:T(512)S(1)}, u32[]{:S(2)}, u32[]{:S(2)}) collective-permute-start(f32[512]{0:T(512)S(1)} %get-tuple-element.118), channel_id=1, source_target_pairs={{0,1},{1,2},{2,3},{3,4},{4,5},{5,6},{6,7},{7,8},{8,9},{9,10},{10,1... | collective-permute-start | bytes 6152 | tf_op jit(solution)/shard_map/while/body/eval_jaxpr/ppermute | solution.py:10
  139.8 8.9 %collective-permute-start.1 = (f32[512,32]{1,0:T(8,128)S(1)}, f32[512,32]{1,0:T(8,128)S(1)}, u32[]{:S(2)}, u32[]{:S(2)}) collective-permute-start(f32[512,32]{1,0:T(8,128)S(1)} %get-tuple-element.117), channel_id=1, source_target_pairs={{0,1},{1,2},{2,3},{3,4},{4,5},{5,6},{6,7},{7,8},{8,9},{9,10},{10,1... | collective-permute-start | bytes 196616 | tf_op jit(solution)/shard_map/while/body/eval_jaxpr/ppermute | solution.py:10
  139.8 8.9 %collective-permute-start = (f32[512,16]{0,1:T(8,128)S(1)}, f32[512,16]{0,1:T(8,128)S(1)}, u32[]{:S(2)}, u32[]{:S(2)}) collective-permute-start(f32[512,16]{0,1:T(8,128)S(1)} %get-tuple-element.119), channel_id=1, source_target_pairs={{0,1},{1,2},{2,3},{3,4},{4,5},{5,6},{6,7},{7,8},{8,9},{9,10},{10,1... | collective-permute-start | bytes 98312 | tf_op jit(solution)/shard_map/while/body/eval_jaxpr/ppermute | solution.py:10
  139.9 8.8 %collective-permute-start.2 = (f32[512]{0:T(512)S(1)}, f32[512]{0:T(512)S(1)}, u32[]{:S(2)}, u32[]{:S(2)}) collective-permute-start(f32[512]{0:T(512)S(1)} %get-tuple-element.118), channel_id=1, source_target_pairs={{0,1},{1,2},{2,3},{3,4},{4,5},{5,6},{6,7},{7,8},{8,9},{9,10},{10,1... | collective-permute-start | bytes 6152 | tf_op jit(solution)/shard_map/while/body/eval_jaxpr/ppermute | solution.py:10
  150.9 8.9 %collective-permute-start.1 = (f32[512,32]{1,0:T(8,128)S(1)}, f32[512,32]{1,0:T(8,128)S(1)}, u32[]{:S(2)}, u32[]{:S(2)}) collective-permute-start(f32[512,32]{1,0:T(8,128)S(1)} %get-tuple-element.117), channel_id=1, source_target_pairs={{0,1},{1,2},{2,3},{3,4},{4,5},{5,6},{6,7},{7,8},{8,9},{9,10},{10,1... | collective-permute-start | bytes 196616 | tf_op jit(solution)/shard_map/while/body/eval_jaxpr/ppermute | solution.py:10
  151.0 8.9 %collective-permute-start = (f32[512,16]{0,1:T(8,128)S(1)}, f32[512,16]{0,1:T(8,128)S(1)}, u32[]{:S(2)}, u32[]{:S(2)}) collective-permute-start(f32[512,16]{0,1:T(8,128)S(1)} %get-tuple-element.119), channel_id=1, source_target_pairs={{0,1},{1,2},{2,3},{3,4},{4,5},{5,6},{6,7},{7,8},{8,9},{9,10},{10,1... | collective-permute-start | bytes 98312 | tf_op jit(solution)/shard_map/while/body/eval_jaxpr/ppermute | solution.py:10
  151.1 8.8 %collective-permute-start.2 = (f32[512]{0:T(512)S(1)}, f32[512]{0:T(512)S(1)}, u32[]{:S(2)}, u32[]{:S(2)}) collective-permute-start(f32[512]{0:T(512)S(1)} %get-tuple-element.118), channel_id=1, source_target_pairs={{0,1},{1,2},{2,3},{3,4},{4,5},{5,6},{6,7},{7,8},{8,9},{9,10},{10,1... | collective-permute-start | bytes 6152 | tf_op jit(solution)/shard_map/while/body/eval_jaxpr/ppermute | solution.py:10
  162.1 9.0 %collective-permute-start.1 = (f32[512,32]{1,0:T(8,128)S(1)}, f32[512,32]{1,0:T(8,128)S(1)}, u32[]{:S(2)}, u32[]{:S(2)}) collective-permute-start(f32[512,32]{1,0:T(8,128)S(1)} %get-tuple-element.117), channel_id=1, source_target_pairs={{0,1},{1,2},{2,3},{3,4},{4,5},{5,6},{6,7},{7,8},{8,9},{9,10},{10,1... | collective-permute-start | bytes 196616 | tf_op jit(solution)/shard_map/while/body/eval_jaxpr/ppermute | solution.py:10
  162.2 8.9 %collective-permute-start = (f32[512,16]{0,1:T(8,128)S(1)}, f32[512,16]{0,1:T(8,128)S(1)}, u32[]{:S(2)}, u32[]{:S(2)}) collective-permute-start(f32[512,16]{0,1:T(8,128)S(1)} %get-tuple-element.119), channel_id=1, source_target_pairs={{0,1},{1,2},{2,3},{3,4},{4,5},{5,6},{6,7},{7,8},{8,9},{9,10},{10,1... | collective-permute-start | bytes 98312 | tf_op jit(solution)/shard_map/while/body/eval_jaxpr/ppermute | solution.py:10
  162.2 8.8 %collective-permute-start.2 = (f32[512]{0:T(512)S(1)}, f32[512]{0:T(512)S(1)}, u32[]{:S(2)}, u32[]{:S(2)}) collective-permute-start(f32[512]{0:T(512)S(1)} %get-tuple-element.118), channel_id=1, source_target_pairs={{0,1},{1,2},{2,3},{3,4},{4,5},{5,6},{6,7},{7,8},{8,9},{9,10},{10,1... | collective-permute-start | bytes 6152 | tf_op jit(solution)/shard_map/while/body/eval_jaxpr/ppermute | solution.py:10
  203.8 30.2 %copy-start.2 = (f32[512,16]{0,1:T(8,128)}, f32[512,16]{0,1:T(8,128)S(1)}, u32[]{:S(2)}) copy-start(f32[512,16]{0,1:T(8,128)S(1)} %get-tuple-element.60) | copy-start | bytes 98308
  (2 other events, 1.7 us)
where the time goes:
time: 234 us
  waiting for transfers between devices  129 us (55%)
  blocking collectives  59 us (25%)
  matrix products  35.2 us (15%)
  starting transfers between devices  5.37 us (2%)
    ppermute x45, waiting for transfers between devices, shifted(): return lax.ppermute(value, axis, pairs)  129 us
    psum x2, blocking collectives, column_norms(): return lax.psum(jnp.sum(residual * residual, axis=0), 'blk')  59 us
    dot_general x16, matrix products, product(): jnp.dot(left, right, precision=lax.Precision.HIGHEST, preferred_element_t...  19.2 us
    dot_general x16, matrix products, kernel_tile(): lax.dot_general(near, far_points, (((1,), (1,)), ((), ())), precision=lax...  16 us
    ppermute x45, starting transfers between devices, shifted(): return lax.ppermute(value, axis, pairs)  5.37 us
  transfers between devices with their start and end apart: 45, of which 15 were waited for; matrix products, arithmetic and copies ran while one was open for 0% of the time, Pallas kernels for 0%

commit v1 on v0

v1 whole, which is shorter than its diff:
```python
import functools

import jax
import jax.numpy as jnp
from jax import lax
from jax.experimental import pallas as pl
from jax.experimental.pallas import tpu as pltpu
from jax.sharding import PartitionSpec as P

F32 = jnp.float32
BF16 = jnp.bfloat16
LOG2E = 1.4426950408889634


def split3(value):
    high = value.astype(BF16)
    rest = value - high.astype(F32)
    middle = rest.astype(BF16)
    low = (rest - middle.astype(F32)).astype(BF16)
    return high, middle, low


def augmented(scaled, near):
    count = scaled.shape[1]
    norm = -0.5 * jnp.sum(scaled * scaled, axis=0, keepdims=True)
    row = lax.broadcasted_iota(jnp.int32, (16, count), 0)
    first = 0 if near else 3
    tail = jnp.where(row < 6, 1.0, 0.0)
    for offset, part in enumerate(split3(norm)):
        spread = jnp.broadcast_to(part.astype(F32), (16, count))
        tail = jnp.where(row == first + offset, spread, tail)
    high, middle, low = split3(scaled)
    if near:
        parts = [high, high, middle, high, low, middle]
    else:
        parts = [high, middle, high, low, high, middle]
    return jnp.concatenate(parts + [tail.astype(BF16)], axis=0)


def kernel(
    n, ladder, points_ref, targets_ref, noise_ref, inv_ref, sol_ref, res_ref, dir_ref,
    held, near, total, mine, stats, send_sem, recv_sem, stat_send, stat_recv,
):
    features, count = points_ref.shape
    columns = targets_ref.shape[0]
    chips = n // 2
    half = chips // 2
    me = lax.axis_index("blk")
    core, chip = lax.rem(me, 2), lax.div(me, 2)

    if ladder:
        side, level = lax.rem(chip, 2), lax.div(chip, 2)
        place = level + side * (chips - 1 - 2 * level)
    else:
        place = chip

    def device_at(place):
        place = lax.rem(place + chips, chips)
        if ladder:
            side = lax.div(place, half)
            level = place + side * (chips - 1 - 2 * place)
            place = 2 * level + side
        return 2 * place + core

    toward = 1 - 2 * core
    ahead = device_at(place + toward)
    behind = device_at(place - toward)
    sibling = 2 * chip + 1 - core

    def copy(source, slot, target):
        return pltpu.make_async_remote_copy(
            src_ref=held.at[source],
            dst_ref=held.at[slot],
            send_sem=send_sem.at[slot],
            recv_sem=recv_sem.at[slot],
            device_id={"blk": target},
            device_id_type=pl.DeviceIdType.MESH,
        )

    def stat_copy(offset):
        return pltpu.make_async_remote_copy(
            src_ref=mine,
            dst_ref=stats.at[offset],
            send_sem=stat_send.at[offset],
            recv_sem=stat_recv.at[offset],
            device_id={"blk": lax.rem(me + offset, n)},
            device_id_type=pl.DeviceIdType.MESH,
        )

    barrier = pltpu.get_barrier_semaphore()

    def greet(offset, _):
        pl.semaphore_signal(
            barrier,
            inc=1,
            device_id={"blk": lax.rem(me + offset, n)},
            device_id_type=pl.DeviceIdType.MESH,
        )
        return 0

    lax.fori_loop(1, n, greet, 0)

    eye = lax.broadcasted_iota(jnp.int32, (features, features), 0) == lax.broadcasted_iota(
        jnp.int32, (features, features), 1
    )
    inv = jnp.sum(jnp.where(eye, inv_ref[...], 0.0), axis=1, keepdims=True)
    held[0, :features] = points_ref[...] * inv * (LOG2E**0.5)
    held[0, features:] = targets_ref[...]
    pl.semaphore_wait(barrier, n - 1)
    copy(0, 2, ahead).start()
    copy(0, 3, behind).start()
    copy(0, 1, sibling).start()
    near[...] = augmented(held[0, :features], True).astype(F32).T.astype(BF16)
    total[...] = jnp.zeros_like(total)

    def visit(slot, _):
        hop = lax.div(slot + 2, 4)
        phase = lax.rem(slot, 4)

        @pl.when(slot > 0)
        def _():
            @pl.when(jnp.logical_or(phase != 3, slot == n - 1))
            def _():
                copy(0, slot, sibling).wait_recv()

            @pl.when(phase == 2)
            def _():
                @pl.when(hop < half)
                def _():
                    copy(slot, slot + 4, ahead).start()
                    copy(slot, slot + 2, sibling).start()
                    copy(0, slot + 1, sibling).wait_recv()

                    @pl.when(hop < half - 1)
                    def _():
                        copy(slot + 1, slot + 5, behind).start()

                    copy(slot + 1, slot + 3, sibling).start()

                @pl.when(hop == half)
                def _():
                    copy(slot, slot + 1, sibling).start()

        block = held[slot]
        far = augmented(block[:features], False)
        vectors = block[features:]
        high = vectors.astype(BF16)
        low = (vectors - high.astype(F32)).astype(BF16)
        pair = jnp.concatenate([high, low], axis=0)
        exponent = jnp.dot(near[...], far, preferred_element_type=F32)
        values = jnp.exp2(exponent)
        upper = values.astype(BF16)
        lower = (values - upper.astype(F32)).astype(BF16)
        contract = (((1,), (1,)), ((), ()))
        total[...] += lax.dot_general(upper, pair, contract, preferred_element_type=F32) + (
            lax.dot_general(lower, pair, contract, preferred_element_type=F32)
        )
        return 0

    lax.fori_loop(0, n, visit, 0)

    summed = total[...].T
    targets = held[0, features:]
    image = summed[:columns] + summed[columns:] + noise_ref[...] * targets

    def over_points(value):
        return jnp.sum(value, axis=1, keepdims=True)

    curvature = over_points(targets * image)
    image_norm = over_points(image * image)
    best = jnp.where(image_norm > 0.0, curvature / jnp.where(image_norm > 0.0, image_norm, 1.0), 0.0)
    rest = targets - best * image
    lane = lax.broadcasted_iota(jnp.int32, mine.shape, 1)
    packed = jnp.zeros(mine.shape, F32)
    for index, value in enumerate(
        (curvature, over_points(targets * targets), over_points(rest * rest), image_norm, best)
    ):
        packed = jnp.where(lane == index, value, packed)
    mine[...] = packed
    stats[0] = packed

    def send(offset, _):
        stat_copy(offset).start()
        return 0

    def receive(offset, _):
        stat_copy(offset).wait_recv()
        return 0

    lax.fori_loop(1, n, send, 0)
    lax.fori_loop(1, n, receive, 0)

    def add(offset, state):
        return state + stats[offset]

    sums = lax.fori_loop(0, n, add, jnp.zeros(mine.shape, F32), unroll=True)
    norm_now = sums[:, 1:2]
    step_size = norm_now / sums[:, 0:1]

    def add_norm(offset, state):
        part = stats[offset]
        gap = step_size - part[:, 4:5]
        return state + (part[:, 2:3] + gap * gap * part[:, 3:4])

    norm_next = lax.fori_loop(0, n, add_norm, jnp.zeros((columns, 1), F32), unroll=True)
    residual = targets - step_size * image
    sol_ref[...] = step_size * targets
    res_ref[...] = residual
    dir_ref[...] = residual + (norm_next / norm_now) * targets

    def finish(slot, _):
        copy(0, slot, sibling).wait_send()
        stat_copy(slot).wait_send()
        return 0

    lax.fori_loop(1, n, finish, 0)


def solution(mesh):
    n = mesh.shape["blk"]
    ladder = mesh.shape["groups"] == 2

    def body(points, targets, noise_var, inv_length):
        count, features = points.shape
        columns = targets.shape[1]
        out = jax.ShapeDtypeStruct((columns, count), F32)
        vmem = pl.BlockSpec(memory_space=pltpu.VMEM)
        outs = pl.pallas_call(
            functools.partial(kernel, n, ladder),
            out_shape=[out] * 3,
            in_specs=[vmem] * 4,
            out_specs=[vmem] * 3,
            scratch_shapes=[
                pltpu.VMEM((n, features + columns, count), F32),
                pltpu.VMEM((count, 6 * features + 16), BF16),
                pltpu.VMEM((count, 2 * columns), F32),
                pltpu.VMEM((columns, 128), F32),
                pltpu.VMEM((n, columns, 128), F32),
                pltpu.SemaphoreType.DMA((n,)),
                pltpu.SemaphoreType.DMA((n,)),
                pltpu.SemaphoreType.DMA((n,)),
                pltpu.SemaphoreType.DMA((n,)),
            ],
            compiler_params=pltpu.CompilerParams(
                collective_id=0, has_side_effects=True, vmem_limit_bytes=40 * 2**20
            ),
        )(points.T, targets.T, noise_var[None, :], inv_length[None, :])
        return tuple(value.T for value in outs)

    rows, flat = P(("groups", "blk"), None), P(("groups", "blk"))
    return jax.shard_map(
        body,
        mesh=mesh,
        in_specs=(rows, rows, flat, P()),
        out_specs=(rows,) * 3,
        check_vma=False,
    )
```

time: 234 us -> 32.9 us (0.14)
  waiting for transfers between devices: 129 us -> 0 us
  blocking collectives: 59 us -> 0 us
  matrix products: 35.2 us -> 0 us
  Pallas kernels: 0 us -> 27.9 us
  starting transfers between devices: 5.37 us -> 0 us
    ppermute x45 -> x0, waiting for transfers between devices: 129 us -> none  [shifted(): return lax.ppermute(value, axis, pairs)]
    psum x2 -> x0, blocking collectives: 59 us -> none  [column_norms(): return lax.psum(jnp.sum(residual * residual, axis=0), 'blk')]
    dot_general x32 -> x0, matrix products: 35.2 us -> none  [the longest x16 19.2 us: product(): jnp.dot(left, right, precision=lax.Precision.HIGHEST, preferred_element_t...]
    pallas_call x0 -> x1, Pallas kernels: none -> 27.9 us  [body(): pl.pallas_call(functools.partial(kernel, n, ladder), out_shape=[out] * 3,...]
    ppermute x45 -> x0, starting transfers between devices: 5.37 us -> none  [shifted(): return lax.ppermute(value, axis, pairs)]
    unnamed x13 -> x11, local copies, waits for them, and re-layouts: 1.77 us -> 4.11 us
  transfers between devices with their start and end apart: 45 -> 0, of which waited for: 15 -> 0; matrix products, arithmetic and copies ran while one was open for 0% -> 0% of each run, Pallas kernels for 0% -> 0%
where the time goes in v1:
time: 32.9 us; the launch traced here: 32.7 us
  Pallas kernels  27.9 us (85%)
  local copies, waits for them, and re-layouts  4.11 us (12%)
  between operations  0.66 us (2%)
    pallas_call x1, Pallas kernels, body(): pl.pallas_call(functools.partial(kernel, n, ladder), out_shape=[out] * 3,...  27.9 us
    unnamed x11, local copies, waits for them, and re-layouts  4.11 us

profile of v1, /device:TPU:0, one launch (start us, length us, event | category | flops | bytes accessed | tf_op | source)
XLA Modules:
  0.0 32.7 jit_solution(157989186004963589)
XLA Ops:
  0.6 0.0 copy-start.2
  0.6 0.0 copy-start.3
  0.7 0.7 %copy-done.2 = f32[512]{0:T(512)S(1)} copy-done((f32[512]{0:T(512)S(1)}, f32[512]{0:T(512)}, u32[]{:S(2)}) %copy-start.2) | copy-done | bytes 2072
  1.3 0.0 copy-done.3
  1.3 0.0 copy-start
  1.3 0.8 %copy-done = f32[512,32]{0,1:T(8,128)S(1)} copy-done((f32[512,32]{0,1:T(8,128)S(1)}, f32[512,32]{0,1:T(8,128)}, u32[]{:S(2)}) %copy-start) | copy-done | bytes 65560
  2.2 0.0 copy-start.1
  2.2 0.8 %copy-done.1 = f32[512,16]{0,1:T(8,128)S(1)} copy-done((f32[512,16]{0,1:T(8,128)S(1)}, f32[512,16]{0,1:T(8,128)}, u32[]{:S(2)}) %copy-start.1) | copy-done | bytes 32792
  2.9 27.9 %shard_map.67 = (f32[16,512]{1,0:T(8,128)S(1)}, f32[16,512]{1,0:T(8,128)S(1)}, f32[16,512]{1,0:T(8,128)S(1)}) custom-call(f32[32,512]{1,0:T(8,128)S(1)} %bitcast.7, f32[16,512]{1,0:T(8,128)S(1)} %bitcast.8, f32[1,512]{1,0:T(1,128)S(1)} %bitcast.12, f32[1,32]{1,0:T(1,128)S(1)} %bitcast.13), custom_call_target="tpu_custom_call" | custom-call | tf_op jit(solution)/shard_map/pallas_call | solution.py:228
  30.8 0.6 %copy.10 = f32[512,16]{0,1:T(8,128)} copy(f32[512,16]{0,1:T(8,128)S(1)} %bitcast.11) | data formatting | bytes 65536
  31.5 0.6 %copy.11 = f32[512,16]{0,1:T(8,128)} copy(f32[512,16]{0,1:T(8,128)S(1)} %bitcast.10) | data formatting | bytes 65536
  32.1 0.6 %copy.12 = f32[512,16]{0,1:T(8,128)} copy(f32[512,16]{0,1:T(8,128)S(1)} %bitcast.9) | data formatting | bytes 65536
Async XLA Ops:
  0.6 0.7 %copy-start.2 = (f32[512]{0:T(512)S(1)}, f32[512]{0:T(512)}, u32[]{:S(2)}) copy-start(f32[512]{0:T(512)} %param.6) | copy-start | bytes 6148
  0.6 0.7 %copy-start.3 = (f32[32]{0:T(128)S(1)}, f32[32]{0:T(128)}, u32[]{:S(2)}) copy-start(f32[32]{0:T(128)} %param.7) | copy-start | bytes 388
  1.3 0.8 %copy-start = (f32[512,32]{0,1:T(8,128)S(1)}, f32[512,32]{0,1:T(8,128)}, u32[]{:S(2)}) copy-start(f32[512,32]{0,1:T(8,128)} %param.4) | copy-start | bytes 196612
  2.2 0.8 %copy-start.1 = (f32[512,16]{0,1:T(8,128)S(1)}, f32[512,16]{0,1:T(8,128)}, u32[]{:S(2)}) copy-start(f32[512,16]{0,1:T(8,128)} %param.5) | copy-start | bytes 98308

commit v2 on v1

v2 whole, which is shorter than its diff:
```python
import functools

import jax
import jax.numpy as jnp
from jax import lax
from jax.experimental import pallas as pl
from jax.experimental.pallas import tpu as pltpu
from jax.sharding import PartitionSpec as P

F32 = jnp.float32
BF16 = jnp.bfloat16
LOG2E = 1.4426950408889634


def split3(value):
    high = value.astype(BF16)
    rest = value - high.astype(F32)
    middle = rest.astype(BF16)
    low = (rest - middle.astype(F32)).astype(BF16)
    return high, middle, low


def augmented(scaled, near):
    count = scaled.shape[1]
    norm = -0.5 * jnp.sum(scaled * scaled, axis=0, keepdims=True)
    row = lax.broadcasted_iota(jnp.int32, (16, count), 0)
    first = 0 if near else 3
    tail = jnp.where(row < 6, 1.0, 0.0)
    for offset, part in enumerate(split3(norm)):
        spread = jnp.broadcast_to(part.astype(F32), (16, count))
        tail = jnp.where(row == first + offset, spread, tail)
    high, middle, low = split3(scaled)
    if near:
        parts = [high, high, middle, high, low, middle]
    else:
        parts = [high, middle, high, low, high, middle]
    return jnp.concatenate(parts + [tail.astype(BF16)], axis=0)


def kernel(
    n, ladder, points_ref, targets_ref, noise_ref, inv_ref, sol_ref, res_ref, dir_ref,
    held, points, noise, inverse, near, total, mine, layer, line,
    send_sem, recv_sem, load_sem, layer_send, layer_recv, line_send, line_recv,
):
    features, count = points_ref.shape
    columns = targets_ref.shape[0]
    width = count // 2
    chips = n // 2
    half = chips // 2
    last = n - 2
    quads = n // 4
    me = lax.axis_index("blk")
    core, chip = lax.rem(me, 2), lax.div(me, 2)
    corner, quad = lax.rem(me, 4), lax.div(me, 4)

    if ladder:
        side, level = lax.rem(chip, 2), lax.div(chip, 2)
        place = level + side * (chips - 1 - 2 * level)
    else:
        place = chip

    def device_at(place):
        place = lax.rem(place + chips, chips)
        if ladder:
            side = lax.div(place, half)
            level = place + side * (chips - 1 - 2 * place)
            place = 2 * level + side
        return 2 * place + core

    toward = 1 - 2 * core
    ahead = device_at(place + toward)
    behind = device_at(place - toward)
    sibling = 2 * chip + 1 - core
    layer_peers = [4 * quad + lax.rem(corner + offset, 4) for offset in range(1, 4)]
    line_peers = [4 * lax.rem(quad + offset, quads) + corner for offset in range(1, quads)]

    def remote(source, target_ref, sent, received, target):
        return pltpu.make_async_remote_copy(
            src_ref=source,
            dst_ref=target_ref,
            send_sem=sent,
            recv_sem=received,
            device_id={"blk": target},
            device_id_type=pl.DeviceIdType.MESH,
        )

    def chunk(unit, part, to_unit, to_part, target):
        index = 2 * to_unit + to_part
        return remote(
            held.at[unit, part], held.at[to_unit, to_part], send_sem.at[index], recv_sem.at[index], target
        )

    def share(unit, to_unit):
        index = 2 * to_unit
        return remote(held.at[unit], held.at[to_unit], send_sem.at[index], recv_sem.at[index], sibling)

    barrier = pltpu.get_barrier_semaphore()
    friends = layer_peers + line_peers
    if not ladder:
        friends = friends + [ahead, behind]
    for friend in friends:
        pl.semaphore_signal(
            barrier, inc=1, device_id={"blk": friend}, device_id_type=pl.DeviceIdType.MESH
        )

    loads = [
        pltpu.make_async_copy(points_ref, points, load_sem.at[0]),
        pltpu.make_async_copy(
            targets_ref.at[:, :width], held.at[0, 0, features:], load_sem.at[1]
        ),
        pltpu.make_async_copy(
            targets_ref.at[:, width:], held.at[0, 1, features:], load_sem.at[2]
        ),
        pltpu.make_async_copy(inv_ref, inverse, load_sem.at[3]),
        pltpu.make_async_copy(noise_ref, noise, load_sem.at[4]),
    ]
    for load in loads:
        load.start()
    total[...] = jnp.zeros_like(total)
    for load in loads:
        load.wait()

    eye = lax.broadcasted_iota(jnp.int32, (features, features), 0) == lax.broadcasted_iota(
        jnp.int32, (features, features), 1
    )
    inv = jnp.sum(jnp.where(eye, inverse[...], 0.0), axis=1, keepdims=True)
    scaled = points[...] * inv * (LOG2E**0.5)
    held[0, 0, :features] = scaled[:, :width]
    held[0, 1, :features] = scaled[:, width:]
    pl.semaphore_wait(barrier, len(friends))
    for part in range(2):
        chunk(0, part, 2 + part, 0, ahead).start()
        chunk(0, part, 2 + part, 1, behind).start()
    share(0, 1).start()
    near[...] = augmented(scaled, True).astype(F32).T.astype(BF16)

    def visit(unit, _):
        hop = lax.div(unit + 2, 4)
        phase = lax.rem(unit + 2, 4)
        ring = jnp.logical_and(jnp.logical_and(phase < 2, unit > 0), unit < n - 1)

        @pl.when(jnp.logical_and(unit > 0, jnp.logical_not(ring)))
        def _():
            share(0, unit).wait_recv()

        @pl.when(ring)
        def _():
            chunk(0, 0, unit, 0, sibling).wait_recv()

            @pl.when(hop < half - 1)
            def _():
                chunk(unit, 0, unit + 4, 0, ahead).start()

            @pl.when(hop == half - 1)
            def _():
                chunk(unit, 0, last, phase, ahead).start()

            chunk(0, 0, unit, 1, sibling).wait_recv()

            @pl.when(hop < half - 1)
            def _():
                chunk(unit, 1, unit + 4, 1, behind).start()

            @pl.when(hop < half)
            def _():
                share(unit, unit + 2).start()

            @pl.when(hop == half)
            def _():
                share(unit, unit + 1).start()

        block = jnp.concatenate([held[unit, 0], held[unit, 1]], axis=1)
        far = augmented(block[:features], False)
        vectors = block[features:]
        high = vectors.astype(BF16)
        low = (vectors - high.astype(F32)).astype(BF16)
        pair = jnp.concatenate([high, low], axis=0)
        exponent = jnp.dot(near[...], far, preferred_element_type=F32)
        values = jnp.exp2(exponent)
        upper = values.astype(BF16)
        lower = (values - upper.astype(F32)).astype(BF16)
        contract = (((1,), (1,)), ((), ()))
        total[...] += lax.dot_general(upper, pair, contract, preferred_element_type=F32) + (
            lax.dot_general(lower, pair, contract, preferred_element_type=F32)
        )
        return 0

    lax.fori_loop(0, n, visit, 0)

    summed = total[...].T
    targets = jnp.concatenate([held[0, 0, features:], held[0, 1, features:]], axis=1)
    image = summed[:columns] + summed[columns:] + noise[...] * targets

    def over_points(value):
        return jnp.sum(value, axis=1, keepdims=True)

    def quotient(top, bottom):
        return jnp.where(bottom > 0.0, top / jnp.where(bottom > 0.0, bottom, 1.0), 0.0)

    lane = lax.broadcasted_iota(jnp.int32, mine.shape, 1)

    def packed(*values):
        result = jnp.zeros(mine.shape, F32)
        for index, value in enumerate(values):
            result = jnp.where(lane == index, value, result)
        return result

    def unpacked(value):
        return [jnp.broadcast_to(value[:, i : i + 1], mine.shape) for i in range(5)]

    def rests_at(step, parts):
        rests = 0.0
        for part in parts:
            gap = step - part[4]
            rests += part[2] + gap * gap * part[3]
        return rests

    def exchange(box, sent, received, peers):
        copies = [
            remote(box.at[0], box.at[offset], sent.at[offset], received.at[offset], peer)
            for offset, peer in enumerate(peers, 1)
        ]
        for copy in copies:
            copy.start()
        for copy in copies:
            copy.wait_recv()
        return copies, [unpacked(box[offset]) for offset in range(len(peers) + 1)]

    curvature = over_points(targets * image)
    image_norm = over_points(image * image)
    best = quotient(curvature, image_norm)
    rest = targets - best * image
    layer[0] = packed(
        curvature, over_points(targets * targets), over_points(rest * rest), image_norm, best
    )
    layer_copies, parts = exchange(layer, layer_send, layer_recv, layer_peers)
    curvature, norm_now, image_norm = [sum(part[i] for part in parts) for i in (0, 1, 3)]
    best = quotient(curvature, image_norm)
    line[0] = packed(curvature, norm_now, rests_at(best, parts), image_norm, best)
    line_copies, parts = exchange(line, line_send, line_recv, line_peers)
    curvature, norm_now = [sum(part[i] for part in parts) for i in (0, 1)]
    step_size = norm_now / curvature
    ratio = (rests_at(step_size, parts) / norm_now)[:, :1]
    step_size = step_size[:, :1]
    residual = targets - step_size * image
    sol_ref[...] = step_size * targets
    res_ref[...] = residual
    dir_ref[...] = residual + ratio * targets

    def finish(unit, _):
        phase = lax.rem(unit + 2, 4)
        ring = jnp.logical_and(phase < 2, unit < n - 1)

        @pl.when(ring)
        def _():
            chunk(0, 0, unit, 0, sibling).wait_send()
            chunk(0, 0, unit, 1, sibling).wait_send()

        @pl.when(jnp.logical_not(ring))
        def _():
            share(0, unit).wait_send()

        return 0

    lax.fori_loop(1, n, finish, 0)
    for copy in layer_copies + line_copies:
        copy.wait_send()


def solution(mesh):
    n = mesh.shape["blk"]
    ladder = mesh.shape["groups"] == 2

    def body(points, targets, noise_var, inv_length):
        count, features = points.shape
        columns = targets.shape[1]
        out = jax.ShapeDtypeStruct((columns, count), F32)
        outs = pl.pallas_call(
            functools.partial(kernel, n, ladder),
            out_shape=[out] * 3,
            in_specs=[pl.BlockSpec(memory_space=pl.ANY)] * 4,
            out_specs=[pl.BlockSpec(memory_space=pltpu.VMEM)] * 3,
            scratch_shapes=[
                pltpu.VMEM((n, 2, features + columns, count // 2), F32),
                pltpu.VMEM((features, count), F32),
                pltpu.VMEM((1, count), F32),
                pltpu.VMEM((1, features), F32),
                pltpu.VMEM((count, 6 * features + 16), BF16),
                pltpu.VMEM((count, 2 * columns), F32),
                pltpu.VMEM((columns, 128), F32),
                pltpu.VMEM((4, columns, 128), F32),
                pltpu.VMEM((n // 4, columns, 128), F32),
                pltpu.SemaphoreType.DMA((2 * n,)),
                pltpu.SemaphoreType.DMA((2 * n,)),
                pltpu.SemaphoreType.DMA((5,)),
                pltpu.SemaphoreType.DMA((4,)),
                pltpu.SemaphoreType.DMA((4,)),
                pltpu.SemaphoreType.DMA((n // 4,)),
                pltpu.SemaphoreType.DMA((n // 4,)),
            ],
            compiler_params=pltpu.CompilerParams(collective_id=0, has_side_effects=True),
        )(points.T, targets.T, noise_var[None, :], inv_length[None, :])
        return tuple(value.T for value in outs)

    rows, flat = P(("groups", "blk"), None), P(("groups", "blk"))
    return jax.shard_map(
        body,
        mesh=mesh,
        in_specs=(rows, rows, flat, P()),
        out_specs=(rows,) * 3,
        check_vma=False,
    )
```

time: 32.9 us -> 31.5 us (0.957)
  local copies, waits for them, and re-layouts: 4.11 us -> 2.77 us
    unnamed x11 -> x7, local copies, waits for them, and re-layouts: 4.11 us -> 2.77 us
where the time goes in v2:
time: 31.5 us; the launch traced here: 31.2 us
  Pallas kernels  27.8 us (88%)
  local copies, waits for them, and re-layouts  2.77 us (9%)
  between operations  0.65 us (2%)
    pallas_call x1, Pallas kernels, body(): pl.pallas_call(functools.partial(kernel, n, ladder), out_shape=[out] * 3,...  27.8 us
    unnamed x7, local copies, waits for them, and re-layouts  2.77 us

profile of v2, /device:TPU:0, one launch (start us, length us, event | category | flops | bytes accessed | tf_op | source)
XLA Modules:
  0.0 31.2 jit_solution(3613373626349671139)
XLA Ops:
  0.6 27.8 %shard_map.67 = (f32[16,512]{1,0:T(8,128)}, f32[16,512]{1,0:T(8,128)}, f32[16,512]{1,0:T(8,128)}) custom-call(f32[32,512]{1,0:T(8,128)} %bitcast.7, f32[16,512]{1,0:T(8,128)} %bitcast.8, f32[1,512]{1,0:T(1,128)} %bitcast.12, f32[1,32]{1,0:T(1,128)} %bitcast.13), custom_call_target="tpu_custom_call" | custom-call | tf_op jit(solution)/shard_map/pallas_call | solution.py:278
  28.5 0.0 copy-start.1
  28.5 1.4 %copy.10 = f32[512,16]{0,1:T(8,128)} copy(f32[512,16]{0,1:T(8,128)} %bitcast.11) | data formatting | bytes 65536
  29.8 0.0 copy-done.1
  29.9 0.0 copy-start
  29.9 0.6 %copy.11 = f32[512,16]{0,1:T(8,128)} copy(f32[512,16]{0,1:T(8,128)S(1)} %bitcast.10) | data formatting | bytes 65536
  30.5 0.2 copy-done
  30.6 0.6 %copy.12 = f32[512,16]{0,1:T(8,128)} copy(f32[512,16]{0,1:T(8,128)S(1)} %bitcast.9) | data formatting | bytes 65536
Async XLA Ops:
  28.5 1.4 %copy-start.1 = (f32[16,512]{1,0:T(8,128)S(1)}, f32[16,512]{1,0:T(8,128)}, u32[]{:S(2)}) copy-start(f32[16,512]{1,0:T(8,128)} %get-tuple-element.7) | copy-start | bytes 98308
  29.9 0.8 %copy-start = (f32[16,512]{1,0:T(8,128)S(1)}, f32[16,512]{1,0:T(8,128)}, u32[]{:S(2)}) copy-start(f32[16,512]{1,0:T(8,128)} %get-tuple-element.8) | copy-start | bytes 98308

commit v3 on v2

--- a/solution.py
+++ b/solution.py
@@ -38,9 +38,9 @@
 
 
 def kernel(
-    n, ladder, points_ref, targets_ref, noise_ref, inv_ref, sol_ref, res_ref, dir_ref,
-    held, points, noise, inverse, near, total, mine, layer, line,
-    send_sem, recv_sem, load_sem, layer_send, layer_recv, line_send, line_recv,
+    n, ladder, points_ref, targets_ref, noise_ref, inv_ref, out_ref,
+    held, points, noise, inverse, near, total, stats,
+    send_sem, recv_sem, load_sem, stat_send, stat_recv,
 ):
     features, count = points_ref.shape
     columns = targets_ref.shape[0]
@@ -48,10 +48,8 @@
     chips = n // 2
     half = chips // 2
     last = n - 2
-    quads = n // 4
     me = lax.axis_index("blk")
     core, chip = lax.rem(me, 2), lax.div(me, 2)
-    corner, quad = lax.rem(me, 4), lax.div(me, 4)
 
     if ladder:
         side, level = lax.rem(chip, 2), lax.div(chip, 2)
@@ -71,8 +69,6 @@
     ahead = device_at(place + toward)
     behind = device_at(place - toward)
     sibling = 2 * chip + 1 - core
-    layer_peers = [4 * quad + lax.rem(corner + offset, 4) for offset in range(1, 4)]
-    line_peers = [4 * lax.rem(quad + offset, quads) + corner for offset in range(1, quads)]
 
     def remote(source, target_ref, sent, received, target):
         return pltpu.make_async_remote_copy(
@@ -95,9 +91,7 @@
         return remote(held.at[unit], held.at[to_unit], send_sem.at[index], recv_sem.at[index], sibling)
 
     barrier = pltpu.get_barrier_semaphore()
-    friends = layer_peers + line_peers
-    if not ladder:
-        friends = friends + [ahead, behind]
+    friends = [ahead, behind, sibling]
     for friend in friends:
         pl.semaphore_signal(
             barrier, inc=1, device_id={"blk": friend}, device_id_type=pl.DeviceIdType.MESH
@@ -128,9 +122,8 @@
     held[0, 0, :features] = scaled[:, :width]
     held[0, 1, :features] = scaled[:, width:]
     pl.semaphore_wait(barrier, len(friends))
-    for part in range(2):
-        chunk(0, part, 2 + part, 0, ahead).start()
-        chunk(0, part, 2 + part, 1, behind).start()
+    chunk(0, 0, 2, 0, ahead).start()
+    chunk(0, 0, 2, 1, behind).start()
     share(0, 1).start()
     near[...] = augmented(scaled, True).astype(F32).T.astype(BF16)
 
@@ -138,6 +131,11 @@
         hop = lax.div(unit + 2, 4)
         phase = lax.rem(unit + 2, 4)
         ring = jnp.logical_and(jnp.logical_and(phase < 2, unit > 0), unit < n - 1)
+
+        @pl.when(unit == 1)
+        def _():
+            chunk(0, 1, 3, 0, ahead).start()
+            chunk(0, 1, 3, 1, behind).start()
 
         @pl.when(jnp.logical_and(unit > 0, jnp.logical_not(ring)))
         def _():
@@ -197,55 +195,54 @@
     def quotient(top, bottom):
         return jnp.where(bottom > 0.0, top / jnp.where(bottom > 0.0, bottom, 1.0), 0.0)
 
-    lane = lax.broadcasted_iota(jnp.int32, mine.shape, 1)
+    shape = stats.shape[1:]
+    lane = lax.broadcasted_iota(jnp.int32, shape, 1)
 
     def packed(*values):
-        result = jnp.zeros(mine.shape, F32)
+        result = jnp.zeros(shape, F32)
         for index, value in enumerate(values):
             result = jnp.where(lane == index, value, result)
         return result
 
     def unpacked(value):
-        return [jnp.broadcast_to(value[:, i : i + 1], mine.shape) for i in range(5)]
-
-    def rests_at(step, parts):
-        rests = 0.0
-        for part in parts:
-            gap = step - part[4]
-            rests += part[2] + gap * gap * part[3]
-        return rests
-
-    def exchange(box, sent, received, peers):
-        copies = [
-            remote(box.at[0], box.at[offset], sent.at[offset], received.at[offset], peer)
-            for offset, peer in enumerate(peers, 1)
-        ]
-        for copy in copies:
-            copy.start()
-        for copy in copies:
-            copy.wait_recv()
-        return copies, [unpacked(box[offset]) for offset in range(len(peers) + 1)]
+        return [jnp.broadcast_to(value[:, i : i + 1], shape) for i in range(5)]
+
+    def stat_copy(offset):
+        return remote(
+            stats.at[0], stats.at[offset], stat_send.at[offset], stat_recv.at[offset], lax.rem(me + offset, n)
+        )
+
+    def stat_start(offset, _):
+        stat_copy(offset).start()
+        return 0
+
+    def stat_wait(offset, _):
+        stat_copy(offset).wait_recv()
+        return 0
 
     curvature = over_points(targets * image)
     image_norm = over_points(image * image)
     best = quotient(curvature, image_norm)
     rest = targets - best * image
-    layer[0] = packed(
+    stats[0] = packed(
         curvature, over_points(targets * targets), over_points(rest * rest), image_norm, best
     )
-    layer_copies, parts = exchange(layer, layer_send, layer_recv, layer_peers)
-    curvature, norm_now, image_norm = [sum(part[i] for part in parts) for i in (0, 1, 3)]
-    best = quotient(curvature, image_norm)
-    line[0] = packed(curvature, norm_now, rests_at(best, parts), image_norm, best)
-    line_copies, parts = exchange(line, line_send, line_recv, line_peers)
-    curvature, norm_now = [sum(part[i] for part in parts) for i in (0, 1)]
-    step_size = norm_now / curvature
-    ratio = (rests_at(step_size, parts) / norm_now)[:, :1]
-    step_size = step_size[:, :1]
+    lax.fori_loop(1, n, stat_start, 0)
+    lax.fori_loop(1, n, stat_wait, 0)
+    parts = [stats[offset] for offset in range(n)]
+    sums = sum(parts)
+    norm_now = sums[:, 1:2]
+    step_size = norm_now / sums[:, :1]
+    wide_step = jnp.broadcast_to(step_size, shape)
+    rests = 0.0
+    for part in parts:
+        gap = wide_step - jnp.broadcast_to(part[:, 4:5], shape)
+        rests += part + gap * gap * jnp.broadcast_to(part[:, 3:4], shape)
+    ratio = rests[:, 2:3] / norm_now
     residual = targets - step_size * image
-    sol_ref[...] = step_size * targets
-    res_ref[...] = residual
-    dir_ref[...] = residual + ratio * targets
+    out_ref[:columns] = step_size * targets
+    out_ref[columns : 2 * columns] = residual
+    out_ref[2 * columns :] = residual + ratio * targets
 
     def finish(unit, _):
         phase = lax.rem(unit + 2, 4)
@@ -263,8 +260,24 @@
         return 0
 
     lax.fori_loop(1, n, finish, 0)
-    for copy in layer_copies + line_copies:
-        copy.wait_send()
+
+    def stat_finish(offset, _):
+        stat_copy(offset).wait_send()
+        return 0
+
+    lax.fori_loop(1, n, stat_finish, 0)
+
+
+def spread(packed_ref, sol_ref, res_ref, dir_ref, sem):
+    columns = sol_ref.shape[0]
+    copies = [
+        pltpu.make_async_copy(packed_ref.at[pl.ds(i * columns, columns)], ref, sem.at[i])
+        for i, ref in enumerate((sol_ref, res_ref, dir_ref))
+    ]
+    for copy in copies:
+        copy.start()
+    for copy in copies:
+        copy.wait()
 
 
 def solution(mesh):
@@ -275,11 +288,11 @@
         count, features = points.shape
         columns = targets.shape[1]
         out = jax.ShapeDtypeStruct((columns, count), F32)
-        outs = pl.pallas_call(
+        packed = pl.pallas_call(
             functools.partial(kernel, n, ladder),
-            out_shape=[out] * 3,
+            out_shape=jax.ShapeDtypeStruct((3 * columns, count), F32),
             in_specs=[pl.BlockSpec(memory_space=pl.ANY)] * 4,
-            out_specs=[pl.BlockSpec(memory_space=pltpu.VMEM)] * 3,
+            out_specs=pl.BlockSpec(memory_space=pltpu.VMEM),
             scratch_shapes=[
                 pltpu.VMEM((n, 2, features + columns, count // 2), F32),
                 pltpu.VMEM((features, count), F32),
@@ -287,19 +300,22 @@
                 pltpu.VMEM((1, features), F32),
                 pltpu.VMEM((count, 6 * features + 16), BF16),
                 pltpu.VMEM((count, 2 * columns), F32),
-                pltpu.VMEM((columns, 128), F32),
-                pltpu.VMEM((4, columns, 128), F32),
-                pltpu.VMEM((n // 4, columns, 128), F32),
+                pltpu.VMEM((n, columns, 128), F32),
                 pltpu.SemaphoreType.DMA((2 * n,)),
                 pltpu.SemaphoreType.DMA((2 * n,)),
                 pltpu.SemaphoreType.DMA((5,)),
-                pltpu.SemaphoreType.DMA((4,)),
-                pltpu.SemaphoreType.DMA((4,)),
-                pltpu.SemaphoreType.DMA((n // 4,)),
-                pltpu.SemaphoreType.DMA((n // 4,)),
+                pltpu.SemaphoreType.DMA((n,)),
+                pltpu.SemaphoreType.DMA((n,)),
             ],
             compiler_params=pltpu.CompilerParams(collective_id=0, has_side_effects=True),
         )(points.T, targets.T, noise_var[None, :], inv_length[None, :])
+        outs = pl.pallas_call(
+            spread,
+            out_shape=[out] * 3,
+            in_specs=[pl.BlockSpec(memory_space=pltpu.VMEM)],
+            out_specs=[pl.BlockSpec(memory_space=pl.ANY)] * 3,
+            scratch_shapes=[pltpu.SemaphoreType.DMA((3,))],
+        )(packed)
         return tuple(value.T for value in outs)
 
     rows, flat = P(("groups", "blk"), None), P(("groups", "blk"))

time: 31.5 us -> 28.2 us (0.90)
  local copies, waits for them, and re-layouts: 2.77 us -> 0 us
  Pallas kernels: 27.8 us -> 27.3 us
    unnamed x7 -> x0, local copies, waits for them, and re-layouts: 2.77 us -> none
    pallas_call x1 -> x2, Pallas kernels: 27.8 us -> 27.3 us  [the longest x1 25.8 us: body(): pl.pallas_call(functools.partial(kernel, n, ladder), out_shape=jax.ShapeD...]
where the time goes in v3:
time: 28.2 us; the launch traced here: 28 us
  Pallas kernels  27.3 us (97%)
  between operations  0.64 us (2%)
    pallas_call x1, Pallas kernels, body(): pl.pallas_call(functools.partial(kernel, n, ladder), out_shape=jax.ShapeD...  25.8 us
    pallas_call x1, Pallas kernels, body(): pl.pallas_call(spread, out_shape=[out] * 3, in_specs=[pl.BlockSpec(memory...  1.55 us

profile of v3, /device:TPU:0, one launch (start us, length us, event | category | flops | bytes accessed | tf_op | source)
XLA Modules:
  0.0 28.0 jit_solution(3099271847365413858)
XLA Ops:
  0.6 25.8 %shard_map.67.packed_ref = f32[48,512]{1,0:T(8,128)} custom-call(f32[32,512]{1,0:T(8,128)} %bitcast.7, f32[16,512]{1,0:T(8,128)} %bitcast.8, f32[1,512]{1,0:T(1,128)} %bitcast.9, f32[1,32]{1,0:T(1,128)} %bitcast.10), custom_call_target="tpu_custom_call" | custom-call | tf_op jit(solution)/shard_map/pallas_call | solution.py:291
  26.4 1.6 %shard_map.68 = (f32[16,512]{1,0:T(8,128)}, f32[16,512]{1,0:T(8,128)}, f32[16,512]{1,0:T(8,128)}) custom-call(f32[48,512]{1,0:T(8,128)} %shard_map.67.packed_ref), custom_call_target="tpu_custom_call" | custom-call | tf_op jit(solution)/shard_map/pallas_call | solution.py:312

commit v4 on v3

--- a/solution.py
+++ b/solution.py
@@ -68,6 +68,7 @@
     toward = 1 - 2 * core
     ahead = device_at(place + toward)
     behind = device_at(place - toward)
+    opposite = device_at(place + half)
     sibling = 2 * chip + 1 - core
 
     def remote(source, target_ref, sent, received, target):
@@ -91,7 +92,7 @@
         return remote(held.at[unit], held.at[to_unit], send_sem.at[index], recv_sem.at[index], sibling)
 
     barrier = pltpu.get_barrier_semaphore()
-    friends = [ahead, behind, sibling]
+    friends = [ahead, behind, sibling, opposite]
     for friend in friends:
         pl.semaphore_signal(
             barrier, inc=1, device_id={"blk": friend}, device_id_type=pl.DeviceIdType.MESH
@@ -149,15 +150,16 @@
             def _():
                 chunk(unit, 0, unit + 4, 0, ahead).start()
 
-            @pl.when(hop == half - 1)
-            def _():
-                chunk(unit, 0, last, phase, ahead).start()
-
             chunk(0, 0, unit, 1, sibling).wait_recv()
 
             @pl.when(hop < half - 1)
             def _():
                 chunk(unit, 1, unit + 4, 1, behind).start()
+
+            @pl.when(unit == 3)
+            def _():
+                chunk(0, 0, last, 0, opposite).start()
+                chunk(0, 1, last, 1, opposite).start()
 
             @pl.when(hop < half)
             def _():

time: 28.2 us -> 31.4 us (1.11)
  Pallas kernels: 27.3 us -> 30.6 us
    pallas_call x1, Pallas kernels: 25.8 us -> 29 us  [body(): pl.pallas_call(functools.partial(kernel, n, ladder), out_shape=jax.ShapeD...]
where the time goes in v4:
time: 31.4 us; the launch traced here: 31.2 us
  Pallas kernels  30.6 us (97%)
  between operations  0.64 us (2%)
    pallas_call x1, Pallas kernels, body(): pl.pallas_call(functools.partial(kernel, n, ladder), out_shape=jax.ShapeD...  29 us
    pallas_call x1, Pallas kernels, body(): pl.pallas_call(spread, out_shape=[out] * 3, in_specs=[pl.BlockSpec(memory...  1.55 us

profile of v4, /device:TPU:0, one launch (start us, length us, event | category | flops | bytes accessed | tf_op | source)
XLA Modules:
  0.0 31.2 jit_solution(945235614633563539)
XLA Ops:
  0.6 29.0 %shard_map.67.packed_ref = f32[48,512]{1,0:T(8,128)} custom-call(f32[32,512]{1,0:T(8,128)} %bitcast.7, f32[16,512]{1,0:T(8,128)} %bitcast.8, f32[1,512]{1,0:T(1,128)} %bitcast.9, f32[1,32]{1,0:T(1,128)} %bitcast.10), custom_call_target="tpu_custom_call" | custom-call | tf_op jit(solution)/shard_map/pallas_call | solution.py:293
  29.7 1.6 %shard_map.68 = (f32[16,512]{1,0:T(8,128)}, f32[16,512]{1,0:T(8,128)}, f32[16,512]{1,0:T(8,128)}) custom-call(f32[48,512]{1,0:T(8,128)} %shard_map.67.packed_ref), custom_call_target="tpu_custom_call" | custom-call | tf_op jit(solution)/shard_map/pallas_call | solution.py:314

commit v5 on v3

--- a/solution.py
+++ b/solution.py
@@ -68,6 +68,7 @@
     toward = 1 - 2 * core
     ahead = device_at(place + toward)
     behind = device_at(place - toward)
+    across = ahead + toward
     sibling = 2 * chip + 1 - core
 
     def remote(source, target_ref, sent, received, target):
@@ -124,18 +125,15 @@
     pl.semaphore_wait(barrier, len(friends))
     chunk(0, 0, 2, 0, ahead).start()
     chunk(0, 0, 2, 1, behind).start()
+    chunk(0, 1, 3, 0, ahead).start()
+    chunk(0, 1, 3, 1, behind).start()
     share(0, 1).start()
     near[...] = augmented(scaled, True).astype(F32).T.astype(BF16)
 
     def visit(unit, _):
         hop = lax.div(unit + 2, 4)
         phase = lax.rem(unit + 2, 4)
-        ring = jnp.logical_and(jnp.logical_and(phase < 2, unit > 0), unit < n - 1)
-
-        @pl.when(unit == 1)
-        def _():
-            chunk(0, 1, 3, 0, ahead).start()
-            chunk(0, 1, 3, 1, behind).start()
+        ring = jnp.logical_and(phase < 2, unit > 0)
 
         @pl.when(jnp.logical_and(unit > 0, jnp.logical_not(ring)))
         def _():
@@ -152,6 +150,7 @@
             @pl.when(hop == half - 1)
             def _():
                 chunk(unit, 0, last, phase, ahead).start()
+                chunk(unit, 0, n - 1, phase, across).start()
 
             chunk(0, 0, unit, 1, sibling).wait_recv()
 
@@ -162,10 +161,6 @@
             @pl.when(hop < half)
             def _():
                 share(unit, unit + 2).start()
-
-            @pl.when(hop == half)
-            def _():
-                share(unit, unit + 1).start()
 
         block = jnp.concatenate([held[unit, 0], held[unit, 1]], axis=1)
         far = augmented(block[:features], False)
@@ -246,7 +241,7 @@
 
     def finish(unit, _):
         phase = lax.rem(unit + 2, 4)
-        ring = jnp.logical_and(phase < 2, unit < n - 1)
+        ring = phase < 2
 
         @pl.when(ring)
         def _():

time: 28.2 us -> 28 us (level)
  no operation moved by 1% of the time
where the time goes in v5:
time: 28 us; the launch traced here: 27.7 us
  Pallas kernels  27.1 us (97%)
  between operations  0.64 us (2%)
    pallas_call x1, Pallas kernels, body(): pl.pallas_call(functools.partial(kernel, n, ladder), out_shape=jax.ShapeD...  25.5 us
    pallas_call x1, Pallas kernels, body(): pl.pallas_call(spread, out_shape=[out] * 3, in_specs=[pl.BlockSpec(memory...  1.55 us

profile of v5, /device:TPU:0, one launch (start us, length us, event | category | flops | bytes accessed | tf_op | source)
XLA Modules:
  0.0 27.7 jit_solution(14146968830860544047)
XLA Ops:
  0.6 25.5 %shard_map.67.packed_ref = f32[48,512]{1,0:T(8,128)} custom-call(f32[32,512]{1,0:T(8,128)} %bitcast.7, f32[16,512]{1,0:T(8,128)} %bitcast.8, f32[1,512]{1,0:T(1,128)} %bitcast.9, f32[1,32]{1,0:T(1,128)} %bitcast.10), custom_call_target="tpu_custom_call" | custom-call | tf_op jit(solution)/shard_map/pallas_call | solution.py:286
  26.2 1.6 %shard_map.68 = (f32[16,512]{1,0:T(8,128)}, f32[16,512]{1,0:T(8,128)}, f32[16,512]{1,0:T(8,128)}) custom-call(f32[48,512]{1,0:T(8,128)} %shard_map.67.packed_ref), custom_call_target="tpu_custom_call" | custom-call | tf_op jit(solution)/shard_map/pallas_call | solution.py:307
